TPU v7x, 256 devices: a whole 4x4x8 slice. The times are simulated.
256 devices in a mesh: dp: 32 (over z_lo, x, core), mp: 8 (over z_hi, y).
Axes of the slice: x: 4, y: 4, z: 8 (z_hi: 2, z_lo: 4; z = z_hi * 4 + z_lo), core: 2. Of those that a mesh axis runs over, the one named last changes fastest.
Arguments:
- tokens: bfloat16 [16384, 128, 128], P('dp', 'mp'), may hold values from -6 to 6
- left_factor: float32 [128, 128, 128], P('mp', 'dp'), may hold values from -0.5 to 0.5
- right_factor: float32 [128, 128, 128], P('mp', 'dp'), may hold values from -0.5 to 0.5
- target: bfloat16 [16384, 128, 128], P('dp', 'mp'), may hold values from -6 to 6
Outputs:
- token_grad: bfloat16 [16384, 128, 128], P('dp', 'mp')
- left_grad: float32 [128, 128, 128], P('mp', 'dp')
- right_grad: float32 [128, 128, 128], P('mp', 'dp')
All inputs are finite; a program needn't handle non-finite values.
Results may differ from a plain program's by a relative error of at most 0.024.
Values may be sent and summed in bfloat16 or wider, within the bound.
A program may use at most 64 MiB of HBM per device.

v0:
```python
import jax
import jax.numpy as jnp
from jax import lax
from jax.sharding import PartitionSpec as P


def per_device(tokens, left_factor, right_factor, target):
    groups = lax.axis_size("mp")
    left_rows = left_factor.astype(jnp.bfloat16)
    right_rows = right_factor.astype(jnp.bfloat16)
    left_all, right_all = (
        lax.all_gather(left_rows, "dp", axis=1, tiled=True),
        lax.all_gather(right_rows, "dp", axis=1, tiled=True),
    )
    pre = jnp.einsum("tbi,bij->tbj", tokens, left_all, preferred_element_type=jnp.float32)
    act = jax.nn.gelu(pre).astype(jnp.bfloat16)
    count, local_b, width = act.shape
    local_j = width // groups
    outgoing = (
        act.reshape(count, local_b, groups, local_j)
        .transpose(2, 0, 3, 1)
        .reshape(groups, count, local_j * local_b)
    )
    arrived = lax.all_to_all(outgoing, "mp", split_axis=0, concat_axis=0, tiled=True)
    perm = (
        arrived.reshape(groups, count, local_j, local_b)
        .transpose(1, 2, 0, 3)
        .reshape(count, local_j, groups * local_b)
    )
    out = jnp.einsum("tjb,jbk->tjk", perm, right_all, preferred_element_type=jnp.float32)
    dout = (out - target.astype(jnp.float32)).astype(jnp.bfloat16)
    right_term = jnp.einsum("tjb,tjk->jbk", perm, dout, preferred_element_type=jnp.float32)
    dperm = jnp.einsum("tjk,jbk->tjb", dout, right_all, preferred_element_type=jnp.float32).astype(
        jnp.bfloat16
    )
    sendback = (
        dperm.reshape(count, local_j, groups, local_b)
        .transpose(2, 0, 1, 3)
        .reshape(groups, count, local_j * local_b)
    )
    returned = lax.all_to_all(sendback, "mp", split_axis=0, concat_axis=0, tiled=True)
    dact = (
        returned.reshape(groups, count, local_j, local_b)
        .transpose(1, 3, 0, 2)
        .reshape(count, local_b, groups * local_j)
    )
    pull = jax.vjp(jax.nn.gelu, pre)[1]
    dpre = pull(dact.astype(jnp.float32))[0].astype(jnp.bfloat16)
    left_term = jnp.einsum("tbi,tbj->bij", tokens, dpre, preferred_element_type=jnp.float32)
    token_grad = jnp.einsum(
        "tbj,bij->tbi", dpre, left_all, preferred_element_type=jnp.float32
    ).astype(jnp.bfloat16)
    left_grad, right_grad = (
        lax.psum_scatter(
            left_term.astype(jnp.bfloat16), "dp", scatter_dimension=1, tiled=True
        ).astype(jnp.float32),
        lax.psum_scatter(
            right_term.astype(jnp.bfloat16), "dp", scatter_dimension=1, tiled=True
        ).astype(jnp.float32),
    )
    return (token_grad, left_grad, right_grad)


def solution(mesh):
    in_specs = (P("dp", "mp", None), P("mp", "dp", None), P("mp", "dp", None), P("dp", "mp", None))
    out_specs = (P("dp", "mp", None), P("mp", "dp", None), P("mp", "dp", None))
    return jax.shard_map(
        per_device, mesh=mesh, in_specs=in_specs, out_specs=out_specs, check_vma=False
    )
```

profile of v0, /device:TPU:1, one launch (start us, length us, event | category | flops | bytes accessed | tf_op | source)
XLA Modules:
  0.0 458.3 jit_solution(16812062617411599719)
XLA Ops:
  8.1 47.1 %all_gather.6 = bf16[16,128,128]{2,0,1:T(8,128)(2,1)S(1)} all-gather(bf16[16,4,128]{2,0,1:T(8,128)(2,1)S(1)} %copy.67), channel_id=1, replica_groups=mesh['dp'=32,'mp'=8] {'dp'}, dimensions={1}, use_global_device_ids=true | all-gather | bytes 540672 | tf_op jit(solution)/shard_map/all_gather | solution.py:12
  55.2 3.9 fusion.11
  59.1 2.6 copy.28
  61.6 8.1 %all-to-all-start = ((bf16[8,512,256]{1,2,0:T(8,128)(2,1)}), bf16[8,512,256]{1,2,0:T(8,128)(2,1)}, u32[]{:S(2)}, u32[]{:S(2)}) async-start(bf16[8,512,256]{1,2,0:T(8,128)(2,1)} %bitcast.61), calls=%async_computation | async-start | bytes 4194304 | tf_op jit(solution)/shard_map/all_to_all | solution.py:24
  69.8 79.4 %all_gather.7 = bf16[16,128,128]{2,0,1:T(8,128)(2,1)S(1)} all-gather(bf16[16,4,128]{2,0,1:T(8,128)(2,1)S(1)} %copy.66), channel_id=1, replica_groups=mesh['dp'=32,'mp'=8] {'dp'}, dimensions={1}, use_global_device_ids=true | all-gather | bytes 540672 | tf_op jit(solution)/shard_map/all_gather | solution.py:13
  149.2 2.0 copy.29
  151.4 1.3 fusion.10
  153.5 1.6 copy.35
  155.0 4.3 all-to-all-start.1
  159.4 2.9 convolution_convert_fusion.1
  162.4 1.1 copy.41
  163.8 41.0 %all-to-all-done.1 = bf16[8,512,256]{1,2,0:T(8,128)(2,1)} async-done(((bf16[8,512,256]{1,2,0:T(8,128)(2,1)}), bf16[8,512,256]{1,2,0:T(8,128)(2,1)}, u32[]{:S(2)}, u32[]{:S(2)}) %all-to-all-start.1) | async-done | bytes 2097184 | tf_op jit(solution)/shard_map/all_to_all | solution.py:41
  204.7 2.2 convert_bitcast_fusion
  206.9 2.4 copy.36
  209.4 3.1 fusion.6
  212.5 1.3 copy-done.3
  213.8 1.2 fusion.19
  215.0 1.2 copy.40
  216.2 93.2 %reduce-scatter.5.cloned.1.call-done = bf16[16,4,128]{2,0,1:T(8,128)(2,1)} async-done(((bf16[16,128,128]{2,0,1:T(8,128)(2,1)}), bf16[16,4,128]{2,0,1:T(8,128)(2,1)}) %reduce-scatter.5.cloned.1.call-update) | async-done | bytes 16400 | tf_op jit(solution)/shard_map/reduce_scatter | solution.py:57
  309.5 1.3 copy.44
  310.8 2.4 convert_bitcast_fusion.1
  313.2 2.7 copy.42
  315.9 134.3 %reduce-scatter.3.cloned.1.call-done = bf16[16,4,128]{2,0,1:T(8,128)(2,1)} async-done(((bf16[16,128,128]{2,0,1:T(8,128)(2,1)}), bf16[16,4,128]{2,0,1:T(8,128)(2,1)}) %reduce-scatter.3.cloned.1.call-update) | async-done | bytes 16400 | tf_op jit(solution)/shard_map/reduce_scatter | solution.py:54
  450.1 1.3 copy.43
  (21 shorter events, 2.2 us)
Async XLA Ops:
  7.2 48.0 %copy-start = (bf16[512,16,128]{2,1,0:T(8,128)(2,1)S(1)}, bf16[512,16,128]{2,1,0:T(8,128)(2,1)}, u32[]{:S(2)}) copy-start(bf16[512,16,128]{2,1,0:T(8,128)(2,1)} %param.4) | copy-start | bytes 6291460
  59.1 10.7 %copy-start.6 = (f32[16,4,128]{2,1,0:T(4,128)S(1)}, f32[16,4,128]{2,1,0:T(4,128)}, u32[]{:S(2)}) copy-start(f32[16,4,128]{2,1,0:T(4,128)} %param.6) | copy-start | bytes 98308
  61.6 87.5 %all-to-all-start = ((bf16[8,512,256]{1,2,0:T(8,128)(2,1)}), bf16[8,512,256]{1,2,0:T(8,128)(2,1)}, u32[]{:S(2)}, u32[]{:S(2)}) async-start(bf16[8,512,256]{1,2,0:T(8,128)(2,1)} %bitcast.61), calls=%async_computation | async-start | bytes 4194304 | tf_op jit(solution)/shard_map/all_to_all | solution.py:24
  149.2 2.2 copy-start.5
  151.2 2.3 copy-start.1
  152.7 2.3 copy-start.2
  155.0 49.7 %all-to-all-start.1 = ((bf16[8,512,256]{1,2,0:T(8,128)(2,1)}), bf16[8,512,256]{1,2,0:T(8,128)(2,1)}, u32[]{:S(2)}, u32[]{:S(2)}) async-start(bf16[8,512,256]{1,2,0:T(8,128)(2,1)} %bitcast.60), calls=%async_computation.1 | async-start | bytes 4194304 | tf_op jit(solution)/shard_map/all_to_all | solution.py:41
  159.4 150.1 %reduce-scatter.5.cloned.1.call-start = ((), (), s32[]{:S(2)}) async-start(), calls=%async_computation.5 | async-start | bytes 540672 | tf_op jit(solution)/shard_map/reduce_scatter | solution.py:57
  163.5 286.6 %reduce-scatter.3.cloned.1.call-start = ((), (), s32[]{:S(2)}) async-start(), calls=%async_computation.4 | async-start | bytes 540672 | tf_op jit(solution)/shard_map/reduce_scatter | solution.py:54
  206.9 2.4 copy-start.4
  212.5 1.3 copy-start.3
Sparse Core Ops, SparseCore 0:
  163.6 145.7 reduce-scatter.4
  312.1 137.9 reduce-scatter.2
where the time goes:
time: 463 us; the launch traced here: 458 us
  waiting for transfers between devices  269 us (58%)
  blocking collectives  126 us (27%)
  local copies, waits for them, and re-layouts  18.7 us (4%)
  between operations  14.2 us (3%)
  starting transfers between devices  12.7 us (3%)
  matrix products  12.4 us (3%)
  other arithmetic  5.28 us (1%)
    reduce_scatter x1, waiting for transfers between devices, per_device(): lax.psum_scatter(left_term.astype(jnp.bfloat16), 'dp', scatter_dimension=...  134 us
    reduce_scatter x1, waiting for transfers between devices, per_device(): lax.psum_scatter(right_term.astype(jnp.bfloat16), 'dp', scatter_dimension...  93.2 us
    all_gather x1, blocking collectives, per_device(): lax.all_gather(right_rows, 'dp', axis=1, tiled=True)  79.4 us
    all_gather x1, blocking collectives, per_device(): lax.all_gather(left_rows, 'dp', axis=1, tiled=True)  47.1 us
    all_to_all x1, waiting for transfers between devices, per_device(): lax.all_to_all(sendback, 'mp', split_axis=0, concat_axis=0, tiled=True)  41 us
  transfers between devices with their start and end apart: 4, of which 3 were waited for; matrix products, arithmetic and copies ran while one was open for 4% of the time, Pallas kernels for 0%

commit v1 on v0

v1 whole, which is shorter than its diff:
```python
import functools

import jax
import jax.numpy as jnp
from jax import lax
from jax.experimental import pallas as pl
from jax.experimental.pallas import tpu as pltpu
from jax.sharding import PartitionSpec as P

MESH = pl.DeviceIdType.MESH
BF, F32 = jnp.bfloat16, jnp.float32
CH = 4
TC = 128
GELU_K = 0.7978845608028654
GELU_C = 0.044715


def mm(a, b):
    return jnp.dot(a, b, preferred_element_type=F32)


def mm_nt(a, b):
    return lax.dot_general(a, b, (((1,), (1,)), ((), ())), preferred_element_type=F32)


def loop(n, body, unroll=1):
    def step(i, carry):
        body(i)
        return carry

    lax.fori_loop(0, n, step, 0, unroll=unroll)


def low_half():
    return lax.broadcasted_iota(jnp.int32, (8, 8, 128), 1) < 4


def kernel(
    tok_hbm, wl_ref, wr_ref, tgt_hbm,
    tg_hbm, lg_out, rg_out,
    tok_raw, tgt_raw, tokT, tgtT, stage, stage2,
    gath, wfull, lw, lwT, rw, rwT,
    gp, fsend, frecv, bsend, brecv, lgrad, rgrad, tgbuf,
    rs0, rs_c, rs1, rs_x, rs2, rs_z,
    in_sem, out_sem, agz_s, agz_r, agx_s, agx_r, agc_s, agc_r,
    f_s, f_r, b_s, b_r, rc_s, rc_r, rx_s, rx_r, rz_s, rz_r,
):
    dp, mp = lax.axis_index("dp"), lax.axis_index("mp")
    z, x, core = dp // 8, lax.rem(dp // 2, 4), lax.rem(dp, 2)

    def z_peer(o):
        return (lax.rem(z + o, 4) * 8 + x * 2 + core, mp)

    def x_peer(o):
        return (z * 8 + lax.rem(x + o, 4) * 2 + core, mp)

    c_peer = (z * 8 + x * 2 + (1 - core), mp)

    def m_peer(o):
        return (dp, lax.rem(mp + o, 8))

    def remote(src, dst, ss, rs, dev):
        return pltpu.make_async_remote_copy(
            src_ref=src, dst_ref=dst, send_sem=ss, recv_sem=rs, device_id=dev, device_id_type=MESH
        )

    def tok_in(c):
        return pltpu.make_async_copy(tok_hbm.at[pl.ds(c * TC, TC)], tok_raw.at[c], in_sem.at[0, c])

    def tgt_in(c):
        return pltpu.make_async_copy(tgt_hbm.at[pl.ds(c * TC, TC)], tgt_raw.at[c], in_sem.at[1, c])

    loop(CH, lambda c: tok_in(c).start())
    loop(CH, lambda c: tgt_in(c).start())

    barrier = pltpu.get_barrier_semaphore()
    peers = [z_peer(o) for o in (1, 2, 3)] + [x_peer(o) for o in (1, 2, 3)] + [c_peer]
    peers += [m_peer(o) for o in range(1, 8)]
    for dev in peers:
        pl.semaphore_signal(barrier, inc=1, device_id=dev, device_id_type=MESH)
    gath[0, core, x, z] = wl_ref[...].astype(BF)
    gath[1, core, x, z] = wr_ref[...].astype(BF)
    pl.semaphore_wait(barrier, len(peers))

    def ag_z(f, o):
        piece = gath.at[f, core, x, z]
        return remote(piece, piece, agz_s.at[f, o - 1], agz_r.at[f, o - 1], z_peer(o))

    def ag_x(f, o):
        piece = gath.at[f, core, x]
        return remote(piece, piece, agx_s.at[f, o - 1], agx_r.at[f, o - 1], x_peer(o))

    def ag_c(f, o):
        piece = gath.at[f, core, lax.rem(x + 4 - o, 4)]
        return remote(piece, piece, agc_s.at[f, o], agc_r.at[f, o], c_peer)

    for f in (0, 1):
        for o in (1, 2, 3):
            ag_z(f, o).start()

    def spread(raw, outT, c):
        stage[...] = raw[c].astype(F32).reshape(TC * 16, 128)

        def one(n):
            rows = stage[pl.ds(n, TC, stride=16), :]
            outT[c, n] = rows.T.astype(BF)

        loop(16, one, 4)

    tok_in(0).wait()
    spread(tok_raw, tokT, 0)
    for f in (0, 1):
        for o in (1, 2, 3):
            ag_z(f, o).wait_recv()
        for o in (1, 2, 3):
            ag_x(f, o).start()
        ag_c(f, 0).start()

    def assemble(f, w, wT):
        def pair(m):
            mx, mz = lax.rem(m, 4), m // 4
            a = gath[f, 0, mx, mz].astype(F32).reshape(8, 8, 128)
            b = gath[f, 1, mx, mz].astype(F32).reshape(8, 8, 128)
            low = low_half()
            rows = pl.ds(pl.multiple_of(m * 8, 8), 8)
            wfull[:, 0, rows, :] = jnp.where(low, a, pltpu.roll(b, 4, 1))
            wfull[:, 1, rows, :] = jnp.where(low, pltpu.roll(a, 4, 1), b)

        loop(16, pair, 2)

        def one(n):
            full = wfull[n // 2, lax.rem(n, 2)]
            w[n] = full.astype(BF)
            wT[n] = full.T.astype(BF)

        loop(16, one, 2)

    def finish_gather(f):
        for o in (1, 2, 3):
            ag_x(f, o).wait_recv()
            ag_c(f, o).start()
        for o in (0, 1, 2, 3):
            ag_c(f, o).wait_recv()

    finish_gather(0)
    assemble(0, lw, lwT)

    def fwd_copy(c, o):
        return remote(
            fsend.at[c, lax.rem(mp + o, 8)], frecv.at[c, mp], f_s.at[c, o - 1], f_r.at[c, o - 1], m_peer(o)
        )

    def bwd_copy(c, o):
        return remote(
            bsend.at[c, lax.rem(mp + o, 8)], brecv.at[c, mp], b_s.at[c, o - 1], b_r.at[c, o - 1], m_peer(o)
        )

    def regroup(src, g, dst):
        for m in range(16):
            dst(m, src[pl.ds(g * 16 + m, 16, stride=128), :].astype(BF))

    def forward(c):
        def one(n):
            pre = mm(lwT[n], tokT[c, n])
            sq = pre * pre
            th = jnp.tanh(pre * (GELU_K + (GELU_K * GELU_C) * sq))
            half = 0.5 + 0.5 * th
            gp[c, n] = half + (0.5 * pre) * (1.0 - th * th) * (GELU_K + (3.0 * GELU_K * GELU_C) * sq)
            stage2[pl.ds(pl.multiple_of(n * 128, 128), 128), :] = pre * half

        loop(16, one, 2)

        def send(i):
            o = i + 1
            g = lax.rem(mp + o, 8)

            def put(m, v):
                fsend[c, g, m] = v

            regroup(stage2, g, put)
            fwd_copy(c, o).start()

        loop(7, send)

        def keep(m, v):
            frecv[c, mp, m] = v

        regroup(stage2, mp, keep)

    forward(0)

    def more(i):
        c = i + 1
        tok_in(c).wait()
        spread(tok_raw, tokT, c)
        forward(c)

    loop(CH - 1, more)

    finish_gather(1)
    assemble(1, rw, rwT)

    def targets(c):
        tgt_in(c).wait()
        spread(tgt_raw, tgtT, c)

    loop(CH, targets)

    lgrad[...] = jnp.zeros_like(lgrad)
    rgrad[...] = jnp.zeros_like(rgrad)

    def right(c):
        loop(7, lambda i: fwd_copy(c, i + 1).wait_recv())

        def one(n):
            act = frecv[c, :, n].reshape(128, TC)
            out = mm(rwT[n], act)
            dout = (out - tgtT[c, n].astype(F32)).astype(BF)
            q, s = n // 2, lax.rem(n, 2)
            rgrad[q, s] = rgrad[q, s] + mm_nt(act, dout)
            stage2[pl.ds(pl.multiple_of(n * 128, 128), 128), :] = mm(rw[n], dout)

        loop(16, one, 2)

        def send(i):
            o = i + 1
            g = lax.rem(mp + o, 8)

            def put(m, v):
                bsend[c, g, m] = v

            regroup(stage2, g, put)
            bwd_copy(c, o).start()

        loop(7, send)

        def keep(m, v):
            brecv[c, mp, m] = v

        regroup(stage2, mp, keep)

    loop(CH, right)

    def pieces(f, grad):
        def pair(m):
            mx, mz = lax.rem(m, 4), m // 4
            rows = pl.ds(pl.multiple_of(m * 8, 8), 8)
            a, b = grad[:, 0, rows, :], grad[:, 1, rows, :]
            low = low_half()
            rs0[f, 0, mx, mz] = jnp.where(low, a, pltpu.roll(b, 4, 1)).reshape(64, 128).astype(BF)
            rs0[f, 1, mx, mz] = jnp.where(low, pltpu.roll(a, 4, 1), b).reshape(64, 128).astype(BF)

        loop(16, pair, 2)

    def rs_core(f):
        return remote(rs0.at[f, 1 - core], rs_c.at[f], rc_s.at[f], rc_r.at[f], c_peer)

    def rs_xx(f, o):
        return remote(
            rs1.at[f, lax.rem(x + o, 4)], rs_x.at[f, o - 1], rx_s.at[f, o - 1], rx_r.at[f, o - 1], x_peer(o)
        )

    def rs_zz(f, o):
        return remote(
            rs2.at[f, lax.rem(z + o, 4)], rs_z.at[f, o - 1], rz_s.at[f, o - 1], rz_r.at[f, o - 1], z_peer(o)
        )

    def rs_start(f, grad):
        pieces(f, grad)
        rs_core(f).start()

    def rs_second(f):
        rs_core(f).wait_recv()

        def add(m):
            mx, mz = m // 4, lax.rem(m, 4)
            rs1[f, mx, mz] = (rs0[f, core, mx, mz].astype(F32) + rs_c[f, mx, mz].astype(F32)).astype(BF)

        loop(16, add, 2)
        for o in (1, 2, 3):
            rs_xx(f, o).start()

    def rs_third(f):
        for o in (1, 2, 3):
            rs_xx(f, o).wait_recv()

        def add(m):
            total = rs1[f, x, m].astype(F32)
            for o in range(3):
                total = total + rs_x[f, o, m].astype(F32)
            rs2[f, m] = total.astype(BF)

        loop(4, add)
        for o in (1, 2, 3):
            rs_zz(f, o).start()

    def rs_last(f, out):
        for o in (1, 2, 3):
            rs_zz(f, o).wait_recv()
        total = rs2[f, z].astype(F32)
        for o in range(3):
            total = total + rs_z[f, o].astype(F32)
        out[...] = total

    def tg_out(c):
        rows = pl.ds(pl.multiple_of(c * TC, TC), TC)
        return pltpu.make_async_copy(tgbuf.at[:, rows, :], tg_hbm.at[:, rows, :], out_sem.at[c])

    def left(c):
        loop(7, lambda i: bwd_copy(c, i + 1).wait_recv())

        def one(n):
            back = brecv[c, :, n].reshape(128, TC).astype(F32)
            dpre = (back * gp[c, n]).astype(BF)
            q, s = n // 2, lax.rem(n, 2)
            lgrad[q, s] = lgrad[q, s] + mm_nt(tokT[c, n], dpre)
            grad = mm(lw[n], dpre)
            tgbuf[n, pl.ds(pl.multiple_of(c * TC, TC), TC), :] = grad.T.astype(BF)

        loop(16, one, 2)
        tg_out(c).start()

    rs_start(1, rgrad)
    left(0)
    rs_second(1)
    left(1)
    rs_third(1)
    left(2)
    rs_last(1, rg_out)
    left(3)
    rs_start(0, lgrad)
    rs_second(0)
    rs_third(0)
    rs_last(0, lg_out)

    for f in (0, 1):
        for o in (1, 2, 3):
            ag_z(f, o).wait_send()
            ag_x(f, o).wait_send()
            rs_xx(f, o).wait_send()
            rs_zz(f, o).wait_send()
        for o in (0, 1, 2, 3):
            ag_c(f, o).wait_send()
        rs_core(f).wait_send()

    def drain(c):
        loop(7, lambda i: fwd_copy(c, i + 1).wait_send())
        loop(7, lambda i: bwd_copy(c, i + 1).wait_send())
        tg_out(c).wait()

    loop(CH, drain)


def step(tokens, left_factor, right_factor, target):
    V = pltpu.VMEM
    D = pltpu.SemaphoreType.DMA
    any_spec = pl.BlockSpec(memory_space=pl.ANY)
    vmem_spec = pl.BlockSpec(memory_space=pltpu.VMEM)
    sq = (128, 128)
    scratch = [
        V((CH, TC, 16, 128), BF), V((CH, TC, 16, 128), BF),
        V((CH, 16, 128, TC), BF), V((CH, 16, 128, TC), BF),
        V((TC * 16, 128), F32), V((16 * 128, TC), F32),
        V((2, 2, 4, 4, 64, 128), BF), V((8, 2) + sq, F32),
        V((16,) + sq, BF), V((16,) + sq, BF), V((16,) + sq, BF), V((16,) + sq, BF),
        V((CH, 16, 128, TC), F32),
        V((CH, 8, 16, 16, TC), BF), V((CH, 8, 16, 16, TC), BF),
        V((CH, 8, 16, 16, TC), BF), V((CH, 8, 16, 16, TC), BF),
        V((8, 2) + sq, F32), V((8, 2) + sq, F32),
        V((16, CH * TC, 128), BF),
        V((2, 2, 4, 4, 64, 128), BF), V((2, 4, 4, 64, 128), BF),
        V((2, 4, 4, 64, 128), BF), V((2, 3, 4, 64, 128), BF),
        V((2, 4, 64, 128), BF), V((2, 3, 64, 128), BF),
        D((2, CH)), D((CH,)),
        D((2, 3)), D((2, 3)), D((2, 3)), D((2, 3)), D((2, 4)), D((2, 4)),
        D((CH, 7)), D((CH, 7)), D((CH, 7)), D((CH, 7)),
        D((2,)), D((2,)), D((2, 3)), D((2, 3)), D((2, 3)), D((2, 3)),
    ]
    tg, lg, rg = pl.pallas_call(
        kernel,
        name="monarch",
        out_shape=(
            jax.ShapeDtypeStruct((16, CH * TC, 128), BF),
            jax.ShapeDtypeStruct((64, 128), F32),
            jax.ShapeDtypeStruct((64, 128), F32),
        ),
        in_specs=[any_spec, vmem_spec, vmem_spec, any_spec],
        out_specs=(any_spec, vmem_spec, vmem_spec),
        scratch_shapes=scratch,
        compiler_params=pltpu.CompilerParams(
            collective_id=0, has_side_effects=True, vmem_limit_bytes=48 << 20
        ),
    )(tokens, left_factor.reshape(64, 128), right_factor.reshape(64, 128), target)
    return tg.transpose(1, 0, 2), lg.reshape(16, 4, 128), rg.reshape(16, 4, 128)


def solution(mesh):
    in_specs = (P("dp", "mp", None), P("mp", "dp", None), P("mp", "dp", None), P("dp", "mp", None))
    out_specs = (P("dp", "mp", None), P("mp", "dp", None), P("mp", "dp", None))
    return jax.shard_map(step, mesh=mesh, in_specs=in_specs, out_specs=out_specs, check_vma=False)
```

time: 463 us -> 142 us (0.31)
  waiting for transfers between devices: 269 us -> 0 us
  Pallas kernels: 0 us -> 134 us
  blocking collectives: 126 us -> 0 us
  between operations: 14.2 us -> 0.65 us
  starting transfers between devices: 12.7 us -> 0 us
  matrix products: 12.4 us -> 0 us
  local copies, waits for them, and re-layouts: 18.7 us -> 7 us
  other arithmetic: 5.28 us -> 0 us
    reduce_scatter x2 -> x0, waiting for transfers between devices: 228 us -> none  [the longest x1 134 us: per_device(): lax.psum_scatter(left_term.astype(jnp.bfloat16), 'dp', scatter_dimension=...]
    pallas_call x0 -> x1, Pallas kernels: none -> 134 us  [step(): pl.pallas_call(kernel, name='monarch', out_shape=(jax.ShapeDtypeStruct((1...]
    all_gather x2 -> x0, blocking collectives: 126 us -> none  [the longest x1 79.4 us: per_device(): lax.all_gather(right_rows, 'dp', axis=1, tiled=True)]
    all_to_all x2 -> x0, waiting for transfers between devices: 41 us -> none  [the longest x1 41 us: per_device(): lax.all_to_all(sendback, 'mp', split_axis=0, concat_axis=0, tiled=True)]
    all_to_all x2 -> x0, starting transfers between devices: 12.5 us -> none  [the longest x1 8.12 us: per_device(): lax.all_to_all(outgoing, 'mp', split_axis=0, concat_axis=0, tiled=True)]
    dot_general x6 -> x0, matrix products: 12.4 us -> none  [the longest x1 3.9 us: per_device(): jnp.einsum('tbi,bij->tbj', tokens, left_all, preferred_element_type=jnp.f...]
    convert_element_type x2 -> x0, other arithmetic: 5.28 us -> none  [per_device(): dpre = pull(dact.astype(jnp.float32))[0].astype(jnp.bfloat16)]
    convert_element_type x3 -> x0, local copies, waits for them, and re-layouts: 4.78 us -> none  [the longest x1 2.43 us: per_device(): dpre = pull(dact.astype(jnp.float32))[0].astype(jnp.bfloat16)]
  transfers between devices with their start and end apart: 4 -> 0, of which waited for: 3 -> 0; matrix products, arithmetic and copies ran while one was open for 4% -> 0% of each run, Pallas kernels for 0% -> 0%
where the time goes in v1:
time: 142 us
  Pallas kernels  134 us (94%)
  local copies, waits for them, and re-layouts  7 us (5%)
    pallas_call x1, Pallas kernels, step(): pl.pallas_call(kernel, name='monarch', out_shape=(jax.ShapeDtypeStruct((1...  134 us
    unnamed x9, local copies, waits for them, and re-layouts  7 us

profile of v1, /device:TPU:1, one launch (start us, length us, event | category | flops | bytes accessed | tf_op | source)
XLA Modules:
  0.0 141.6 jit_solution(3741335367115709591)
XLA Ops:
  0.6 0.0 copy-start
  0.6 1.6 %copy-done = bf16[512,16,128]{2,1,0:T(8,128)(2,1)S(1)} copy-done((bf16[512,16,128]{2,1,0:T(8,128)(2,1)S(1)}, bf16[512,16,128]{2,1,0:T(8,128)(2,1)}, u32[]{:S(2)}) %copy-start) | copy-done | bytes 2097176
  2.2 0.0 copy-start.1
  2.2 0.8 copy-done.1
  3.0 0.0 copy-start.2
  3.0 0.8 copy-done.2
  3.7 134.0 %monarch.1 = (bf16[16,512,128]{2,1,0:T(8,128)(2,1)S(1)}, f32[64,128]{1,0:T(8,128)S(1)}, f32[64,128]{1,0:T(8,128)S(1)}) custom-call(bf16[512,16,128]{2,1,0:T(8,128)(2,1)S(1)} %copy-done, f32[64,128]{1,0:T(8,128)S(1)} %bitcast.6, f32[64,128]{1,0:T(8,128)S(1)} %bitcast.7, bf16[512,16,128]{2,1,0:T(8,128)(2,1)} %tgt_hbm.1), custom_call_target="tpu_custom_call" | custom-call | tf_op jit(solution)/shard_map/monarch/pallas_call | solution.py:379
  137.7 2.7 %copy.7 = bf16[512,16,128]{2,1,0:T(8,128)(2,1)} copy(bf16[512,16,128]{2,0,1:T(8,128)(2,1)S(1)} %bitcast.5) | data formatting | bytes 4194304
  140.4 0.6 copy.10
  141.0 0.6 copy.11
Async XLA Ops:
  0.6 1.6 %copy-start = (bf16[512,16,128]{2,1,0:T(8,128)(2,1)S(1)}, bf16[512,16,128]{2,1,0:T(8,128)(2,1)}, u32[]{:S(2)}) copy-start(bf16[512,16,128]{2,1,0:T(8,128)(2,1)} %tok_hbm.1) | copy-start | bytes 6291460
  2.2 0.8 copy-start.1
  3.0 0.8 copy-start.2

commit v2 on v0

v2 whole, which is shorter than its diff:
```python
import jax
import jax.numpy as jnp
from jax import lax
from jax.experimental import pallas as pl
from jax.experimental.pallas import tpu as pltpu
from jax.sharding import PartitionSpec as P

MESH = pl.DeviceIdType.MESH
BF, F32 = jnp.bfloat16, jnp.float32
CH = 4
TC = 128
LAST = CH - 1
GELU_K = 0.7978845608028654
GELU_C = 0.044715


def mm(a, b):
    return jnp.dot(a, b, preferred_element_type=F32)


def mm_nt(a, b):
    return lax.dot_general(a, b, (((1,), (1,)), ((), ())), preferred_element_type=F32)


def loop(lo, hi, body, unroll=1):
    def step(i, carry):
        body(i)
        return carry

    lax.fori_loop(lo, hi, step, 0, unroll=unroll)


def aligned(i, size):
    return pl.ds(pl.multiple_of(i * size, size), size)


def low_half():
    return lax.broadcasted_iota(jnp.int32, (1, 8, 128), 1) < 4


def kernel(
    tok_hbm, wl_hbm, wr_hbm, tgt_hbm,
    tg_out, lg_out, rg_out,
    tok_raw, tgt_raw, w_raw, tokT, tgtT, stage, stage2, stage3,
    gath, wfull, lw, lwT, rw, rwT,
    gp, fsend, frecv, bsend, brecv, lgrad, rgrad,
    rs0, rs_x, rs2, rs_z,
    in_sem, w_sem, agz_s, agz_r, agx_s, agx_r, agc_s, agc_r,
    f_s, f_r, b_s, b_r, q_s, q_r, rx_s, rx_r, rz_s, rz_r, qx_s, qx_r, qz_s, qz_r,
):
    dp, mp = lax.axis_index("dp"), lax.axis_index("mp")
    z, x, core = dp // 8, lax.rem(dp // 2, 4), lax.rem(dp, 2)
    hi, y = mp // 4, lax.rem(mp, 4)

    def z_peer(o):
        return (lax.rem(z + o, 4) * 8 + x * 2 + core, mp)

    def xc_of(k):
        return lax.rem(x + lax.rem(k, 4), 4), lax.rem(core + k // 4, 2)

    def xc_peer(k):
        px, pc = xc_of(k)
        return (z * 8 + px * 2 + pc, mp)

    def m_of(k):
        return lax.rem(hi + k // 4, 2) * 4 + lax.rem(y + lax.rem(k, 4), 4)

    def remote(src, dst, ss, rs, dev):
        return pltpu.make_async_remote_copy(
            src_ref=src, dst_ref=dst, send_sem=ss, recv_sem=rs, device_id=dev, device_id_type=MESH
        )

    barrier = pltpu.get_barrier_semaphore()
    peers = [z_peer(o) for o in (1, 2, 3)] + [xc_peer(k) for k in range(1, 8)]
    peers += [(dp, m_of(k)) for k in range(1, 8)]
    for dev in peers:
        pl.semaphore_signal(barrier, inc=1, device_id=dev, device_id_type=MESH)

    def w_in(f):
        return pltpu.make_async_copy((wl_hbm, wr_hbm)[f], w_raw.at[f], w_sem.at[f])

    def tok_in(c):
        return pltpu.make_async_copy(tok_hbm.at[aligned(c, TC)], tok_raw.at[c], in_sem.at[0, c])

    def tgt_in(c):
        return pltpu.make_async_copy(tgt_hbm.at[aligned(c, TC)], tgt_raw.at[c], in_sem.at[1, c])

    for f in (0, 1):
        w_in(f).start()
    loop(0, CH, lambda c: tok_in(c).start())
    loop(0, CH, lambda c: tgt_in(c).start())
    for f in (0, 1):
        w_in(f).wait()
        for h in (0, 1):
            gath[f, h, core, x, z] = w_raw[f, 32 * h : 32 * h + 32].astype(BF)
    pl.semaphore_wait(barrier, len(peers))

    def ag_z(f, h, o):
        piece = gath.at[f, h, core, x, z]
        return remote(piece, piece, agz_s.at[f, h, o - 1], agz_r.at[f, h, o - 1], z_peer(o))

    def ag_x(f, h, o):
        piece = gath.at[f, h, core, x]
        return remote(piece, piece, agx_s.at[f, h, o - 1], agx_r.at[f, h, o - 1], xc_peer(o))

    def ag_c(f, h, o):
        piece = gath.at[f, h, core, lax.rem(x + 4 - o, 4)]
        return remote(piece, piece, agc_s.at[f, h, o], agc_r.at[f, h, o], xc_peer(4))

    def gather_first(f, h):
        for o in (1, 2, 3):
            ag_z(f, h, o).start()

    def gather_second(f, h):
        for o in (1, 2, 3):
            ag_z(f, h, o).wait_recv()
        for o in (1, 2, 3):
            ag_x(f, h, o).start()
        ag_c(f, h, 0).start()

    def gather_third(f, h):
        for o in (1, 2, 3):
            ag_x(f, h, o).wait_recv()
            ag_c(f, h, o).start()

    def gather_end(f, h):
        for o in (0, 1, 2, 3):
            ag_c(f, h, o).wait_recv()

    def spread(raw, outT, c):
        stage[...] = raw[c].astype(F32).reshape(TC * 16, 128)

        def one(n):
            rows = stage[pl.ds(n, TC, stride=16), :]
            outT[c, n] = rows.T.astype(BF)

        loop(0, 16, one, 4)

    def tokens_ready(c):
        tok_in(c).wait()
        spread(tok_raw, tokT, c)

    def targets_ready(c):
        tgt_in(c).wait()
        spread(tgt_raw, tgtT, c)

    def assemble(f, h, w, wT):
        def pair(m):
            mx, mz = lax.rem(m, 4), m // 4
            a = gath[f, h, 0, mx, mz].astype(F32).reshape(4, 8, 128)
            b = gath[f, h, 1, mx, mz].astype(F32).reshape(4, 8, 128)
            low = low_half()
            rows = aligned(m, 8)
            wfull[4 * h : 4 * h + 4, 0, rows, :] = jnp.where(low, a, pltpu.roll(b, 4, 1))
            wfull[4 * h : 4 * h + 4, 1, rows, :] = jnp.where(low, pltpu.roll(a, 4, 1), b)

        loop(0, 16, pair, 4)

        def one(n):
            full = wfull[n // 2, lax.rem(n, 2)]
            w[n] = full.astype(BF)
            wT[n] = full.T.astype(BF)

        loop(8 * h, 8 * h + 8, one, 4)

    def fwd_copy(c, k):
        return remote(
            fsend.at[c, m_of(k)], frecv.at[c, mp], f_s.at[c, k - 1], f_r.at[c, k - 1], (dp, m_of(k))
        )

    def bwd_copy(c, k):
        return remote(
            bsend.at[c, m_of(k)], brecv.at[c, mp], b_s.at[c, k - 1], b_r.at[c, k - 1], (dp, m_of(k))
        )

    def quarter_copy(q, k):
        part = pl.ds(4 * q, 4)
        return remote(
            bsend.at[LAST, m_of(k), part], brecv.at[LAST, mp, part],
            q_s.at[q, k - 1], q_r.at[q, k - 1], (dp, m_of(k)),
        )

    def regroup(src, g, m):
        return src[pl.ds(g * 16 + m, 16, stride=128), :].astype(BF)

    def forward_part(c, jh, lo, hi_n):
        rows = aligned(jh, 64)

        def one(n):
            pre = mm(lwT[n, rows, :], tokT[c, n])
            sq = pre * pre
            th = jnp.tanh(pre * (GELU_K + (GELU_K * GELU_C) * sq))
            half = 0.5 + 0.5 * th
            gp[c, n, rows, :] = half + (0.5 * pre) * (1.0 - th * th) * (
                GELU_K + (3.0 * GELU_K * GELU_C) * sq
            )
            stage2[pl.ds(pl.multiple_of(n * 128 + jh * 64, 64), 64), :] = pre * half

        loop(lo, hi_n, one, 4)

    def forward_send(c, lo, hi_k):
        def send(k):
            g = m_of(k)
            for m in range(16):
                fsend[c, g, m] = regroup(stage2, g, m)
            fwd_copy(c, k).start()

        loop(lo, hi_k, send)

    def forward_rest(c):
        forward_part(c, hi, 0, 16)
        forward_send(c, 1, 4)
        for m in range(16):
            frecv[c, mp, m] = regroup(stage2, mp, m)

    for h in (0, 1):
        gather_first(0, h)
    tokens_ready(0)
    for h in (0, 1):
        gather_second(0, h)
    for h in (0, 1):
        gather_first(1, h)
    tokens_ready(1)
    for h in (0, 1):
        gather_third(0, h)
    for h in (0, 1):
        gather_second(1, h)
    for h in (0, 1):
        gather_end(0, h)
        assemble(0, h, lw, lwT)
        forward_part(0, 1 - hi, 8 * h, 8 * h + 8)
    forward_send(0, 4, 8)
    forward_rest(0)

    def forward(c):
        forward_part(c, 1 - hi, 0, 16)
        forward_send(c, 4, 8)
        forward_rest(c)

    forward(1)
    for h in (0, 1):
        gather_third(1, h)

    for h in (0, 1):
        gather_end(1, h)
        assemble(1, h, rw, rwT)

    lgrad[...] = jnp.zeros_like(lgrad)
    rgrad[...] = jnp.zeros_like(rgrad)

    def right(c):
        def one(n):
            act = frecv[c, :, n].reshape(128, TC)
            out = mm(rwT[n], act)
            dout = (out - tgtT[c, n].astype(F32)).astype(BF)
            q, s = n // 2, lax.rem(n, 2)
            rgrad[q, s] = rgrad[q, s] + mm_nt(act, dout)
            stage2[aligned(n, 128), :] = mm(rw[n], dout)

        loop(0, 16, one, 4)
        for m in range(16):
            brecv[c, mp, m] = regroup(stage2, mp, m)

        def fill(k):
            g = m_of(k)
            for m in range(16):
                bsend[c, g, m] = regroup(stage2, g, m)

        loop(1, 8, fill)

    def first(i):
        return lax.rem(i + 3, 7) + 1

    def send_back(c):
        loop(0, 7, lambda i: bwd_copy(c, first(i)).start())

    def turn(c):
        targets_ready(c)
        loop(1, 8, lambda k: fwd_copy(c, k).wait_recv())

        @pl.when(c < 2)
        def _():
            tokens_ready(c + 2)
            forward(c + 2)

        @pl.when(c == 2)
        def _():
            send_back(1)

        right(c)

        @pl.when(c == 0)
        def _():
            send_back(0)

        @pl.when(c == 2)
        def _():
            loop(1, 8, lambda k: bwd_copy(0, k).wait_recv())
            send_back(2)

    loop(0, CH, turn)

    def send_quarter(q):
        loop(0, 7, lambda i: quarter_copy(q, first(i)).start())

    def pieces(f, q, grad):
        def pair(m):
            mx, mz = lax.rem(m, 4), m // 4
            rows = aligned(m, 8)
            a, b = grad[2 * q : 2 * q + 2, 0, rows, :], grad[2 * q : 2 * q + 2, 1, rows, :]
            low = low_half()
            rs0[f, 0, mx, q, mz] = jnp.where(low, a, pltpu.roll(b, 4, 1)).reshape(16, 128).astype(BF)
            rs0[f, 1, mx, q, mz] = jnp.where(low, pltpu.roll(a, 4, 1), b).reshape(16, 128).astype(BF)

        loop(0, 16, pair, 4)

    def add_first(f, q):
        for m in range(4):
            total = rs0[f, core, x, q, m].astype(F32)
            for k in range(7):
                total = total + rs_x[f, k, q, m].astype(F32)
            rs2[f, m, q] = total.astype(BF)

    def add_last(f, q, out):
        total = rs2[f, z, q].astype(F32)
        for o in range(3):
            total = total + rs_z[f, o, q].astype(F32)
        out[16 * q : 16 * q + 16, :] = total

    def rx_copy(k):
        px, pc = xc_of(k)
        return remote(rs0.at[1, pc, px], rs_x.at[1, k - 1], rx_s.at[k - 1], rx_r.at[k - 1], xc_peer(k))

    def rz_copy(o):
        return remote(
            rs2.at[1, lax.rem(z + o, 4)], rs_z.at[1, o - 1], rz_s.at[o - 1], rz_r.at[o - 1], z_peer(o)
        )

    def qx_copy(q, k):
        px, pc = xc_of(k)
        return remote(
            rs0.at[0, pc, px, q], rs_x.at[0, k - 1, q], qx_s.at[q, k - 1], qx_r.at[q, k - 1], xc_peer(k)
        )

    def qz_copy(q, o):
        return remote(
            rs2.at[0, lax.rem(z + o, 4), q], rs_z.at[0, o - 1, q],
            qz_s.at[q, o - 1], qz_r.at[q, o - 1], z_peer(o),
        )

    def left_part(c, lo, hi_n):
        def one(n):
            back = brecv[c, :, n].reshape(128, TC).astype(F32)
            dpre = (back * gp[c, n]).astype(BF)
            q, s = n // 2, lax.rem(n, 2)
            lgrad[q, s] = lgrad[q, s] + mm_nt(tokT[c, n], dpre)
            stage3[pl.ds(n, TC, stride=16), :] = mm(lw[n], dpre).T

        loop(lo, hi_n, one, 4)

    def left_out(c):
        def some(i):
            rows = stage3[aligned(i, 256), :].astype(BF).reshape(16, 16, 128)
            tg_out[pl.ds(c * TC + i * 16, 16)] = rows

        loop(0, 8, some)

    def left(c):
        left_part(c, 0, 16)
        left_out(c)

    for q in range(4):
        pieces(1, q, rgrad)
    loop(1, 8, lambda k: rx_copy(k).start())
    left(0)
    loop(1, 8, lambda k: bwd_copy(1, k).wait_recv())
    send_quarter(0)
    send_quarter(1)
    loop(1, 8, lambda k: rx_copy(k).wait_recv())
    for q in range(4):
        add_first(1, q)
    for o in (1, 2, 3):
        rz_copy(o).start()
    left(1)
    loop(1, 8, lambda k: bwd_copy(2, k).wait_recv())
    send_quarter(2)
    left(2)
    for o in (1, 2, 3):
        rz_copy(o).wait_recv()
    for q in range(4):
        add_last(1, q, rg_out)

    def quarter(q):
        loop(1, 8, lambda k: quarter_copy(q, k).wait_recv())
        if q == 0:
            send_quarter(3)
        left_part(LAST, 4 * q, 4 * q + 4)
        pieces(0, q, lgrad)
        loop(1, 8, lambda k: qx_copy(q, k).start())

    def second(q):
        loop(1, 8, lambda k: qx_copy(q, k).wait_recv())
        add_first(0, q)
        for o in (1, 2, 3):
            qz_copy(q, o).start()

    quarter(0)
    quarter(1)
    second(0)
    quarter(2)
    second(1)
    quarter(3)
    second(2)
    left_out(LAST)
    second(3)
    for q in range(4):
        for o in (1, 2, 3):
            qz_copy(q, o).wait_recv()
        add_last(0, q, lg_out)

    for f in (0, 1):
        for h in (0, 1):
            for o in (1, 2, 3):
                ag_z(f, h, o).wait_send()
                ag_x(f, h, o).wait_send()
            for o in (0, 1, 2, 3):
                ag_c(f, h, o).wait_send()
    loop(1, 8, lambda k: rx_copy(k).wait_send())
    for o in (1, 2, 3):
        rz_copy(o).wait_send()

    def drain(c):
        loop(1, 8, lambda k: fwd_copy(c, k).wait_send())

    loop(0, CH, drain)

    def drain_back(c):
        loop(1, 8, lambda k: bwd_copy(c, k).wait_send())

    loop(0, LAST, drain_back)

    def drain_quarter(q):
        loop(1, 8, lambda k: quarter_copy(q, k).wait_send())
        loop(1, 8, lambda k: qx_copy(q, k).wait_send())
        for o in (1, 2, 3):
            qz_copy(q, o).wait_send()

    loop(0, 4, drain_quarter)


def step(tokens, left_factor, right_factor, target):
    V = pltpu.VMEM
    D = pltpu.SemaphoreType.DMA
    hbm = pl.BlockSpec(memory_space=pltpu.HBM)
    vmem = pl.BlockSpec(memory_space=pltpu.VMEM)
    sq = (128, 128)
    scratch = [
        V((CH, TC, 16, 128), BF), V((CH, TC, 16, 128), BF), V((2, 64, 128), F32),
        V((CH, 16, 128, TC), BF), V((CH, 16, 128, TC), BF),
        V((TC * 16, 128), F32), V((16 * 128, TC), F32), V((TC * 16, 128), F32),
        V((2, 2, 2, 4, 4, 32, 128), BF), V((8, 2) + sq, F32),
        V((16,) + sq, BF), V((16,) + sq, BF), V((16,) + sq, BF), V((16,) + sq, BF),
        V((CH, 16, 128, TC), F32),
        V((CH, 8, 16, 16, TC), BF), V((CH, 8, 16, 16, TC), BF),
        V((CH, 8, 16, 16, TC), BF), V((CH, 8, 16, 16, TC), BF),
        V((8, 2) + sq, F32), V((8, 2) + sq, F32),
        V((2, 2, 4, 4, 4, 16, 128), BF), V((2, 7, 4, 4, 16, 128), BF),
        V((2, 4, 4, 16, 128), BF), V((2, 3, 4, 16, 128), BF),
        D((2, CH)), D((2,)),
        D((2, 2, 3)), D((2, 2, 3)), D((2, 2, 3)), D((2, 2, 3)), D((2, 2, 4)), D((2, 2, 4)),
        D((CH, 7)), D((CH, 7)), D((CH, 7)), D((CH, 7)), D((4, 7)), D((4, 7)),
        D((7,)), D((7,)), D((3,)), D((3,)), D((4, 7)), D((4, 7)), D((4, 3)), D((4, 3)),
    ]
    tg, lg, rg = pl.pallas_call(
        kernel,
        name="monarch",
        out_shape=(
            jax.ShapeDtypeStruct((CH * TC, 16, 128), BF),
            jax.ShapeDtypeStruct((64, 128), F32),
            jax.ShapeDtypeStruct((64, 128), F32),
        ),
        in_specs=[hbm, hbm, hbm, hbm],
        out_specs=(vmem, vmem, vmem),
        scratch_shapes=scratch,
        compiler_params=pltpu.CompilerParams(
            collective_id=0, has_side_effects=True, vmem_limit_bytes=51 << 20
        ),
    )(tokens, left_factor.reshape(64, 128), right_factor.reshape(64, 128), target)
    return tg, lg.reshape(16, 4, 128), rg.reshape(16, 4, 128)


def solution(mesh):
    in_specs = (P("dp", "mp", None), P("mp", "dp", None), P("mp", "dp", None), P("dp", "mp", None))
    out_specs = (P("dp", "mp", None), P("mp", "dp", None), P("mp", "dp", None))
    return jax.shard_map(step, mesh=mesh, in_specs=in_specs, out_specs=out_specs, check_vma=False)
```

time: 463 us -> 138 us (0.30)
  waiting for transfers between devices: 269 us -> 0 us
  Pallas kernels: 0 us -> 133 us
  blocking collectives: 126 us -> 0 us
  local copies, waits for them, and re-layouts: 18.7 us -> 4.06 us
  between operations: 14.2 us -> 0.65 us
  starting transfers between devices: 12.7 us -> 0 us
  matrix products: 12.4 us -> 0 us
  other arithmetic: 5.28 us -> 0 us
    reduce_scatter x2 -> x0, waiting for transfers between devices: 228 us -> none  [the longest x1 134 us: per_device(): lax.psum_scatter(left_term.astype(jnp.bfloat16), 'dp', scatter_dimension=...]
    pallas_call x0 -> x1, Pallas kernels: none -> 133 us  [step(): pl.pallas_call(kernel, name='monarch', out_shape=(jax.ShapeDtypeStruct((C...]
    all_gather x2 -> x0, blocking collectives: 126 us -> none  [the longest x1 79.4 us: per_device(): lax.all_gather(right_rows, 'dp', axis=1, tiled=True)]
    all_to_all x2 -> x0, waiting for transfers between devices: 41 us -> none  [the longest x1 41 us: per_device(): lax.all_to_all(sendback, 'mp', split_axis=0, concat_axis=0, tiled=True)]
    all_to_all x2 -> x0, starting transfers between devices: 12.5 us -> none  [the longest x1 8.12 us: per_device(): lax.all_to_all(outgoing, 'mp', split_axis=0, concat_axis=0, tiled=True)]
    dot_general x6 -> x0, matrix products: 12.4 us -> none  [the longest x1 3.9 us: per_device(): jnp.einsum('tbi,bij->tbj', tokens, left_all, preferred_element_type=jnp.f...]
    convert_element_type x2 -> x0, other arithmetic: 5.28 us -> none  [per_device(): dpre = pull(dact.astype(jnp.float32))[0].astype(jnp.bfloat16)]
    convert_element_type x3 -> x0, local copies, waits for them, and re-layouts: 4.78 us -> none  [the longest x1 2.43 us: per_device(): dpre = pull(dact.astype(jnp.float32))[0].astype(jnp.bfloat16)]
  transfers between devices with their start and end apart: 4 -> 0, of which waited for: 3 -> 0; matrix products, arithmetic and copies ran while one was open for 4% -> 0% of each run, Pallas kernels for 0% -> 0%
where the time goes in v2:
time: 138 us; the launch traced here: 137 us
  Pallas kernels  133 us (96%)
  local copies, waits for them, and re-layouts  4.06 us (3%)
    pallas_call x1, Pallas kernels, step(): pl.pallas_call(kernel, name='monarch', out_shape=(jax.ShapeDtypeStruct((C...  133 us
    unnamed x7, local copies, waits for them, and re-layouts  4.06 us

profile of v2, /device:TPU:1, one launch (start us, length us, event | category | flops | bytes accessed | tf_op | source)
XLA Modules:
  0.0 137.4 jit_solution(15100223186383274446)
XLA Ops:
  0.6 0.0 copy-start
  0.6 0.7 copy-done
  1.4 0.0 copy-start.1
  1.4 0.8 copy-done.1
  2.1 132.7 %monarch.1 = (bf16[512,16,128]{2,1,0:T(8,128)(2,1)S(1)}, f32[64,128]{1,0:T(8,128)S(1)}, f32[64,128]{1,0:T(8,128)S(1)}) custom-call(bf16[512,16,128]{2,1,0:T(8,128)(2,1)} %tok_hbm.1, f32[64,128]{1,0:T(8,128)S(1)} %bitcast.4, f32[64,128]{1,0:T(8,128)S(1)} %bitcast.5, bf16[512,16,128]{2,1,0:T(8,128)(2,1)} %tgt_hbm.1), custom_call_target="tpu_custom_call" | custom-call | tf_op jit(solution)/shard_map/monarch/pallas_call | solution.py:474
  134.9 1.3 copy.10
  136.2 0.6 copy.11
  136.8 0.6 copy.12
Async XLA Ops:
  0.6 0.8 copy-start
  1.4 0.8 copy-start.1

commit v3 on v2

--- a/solution.py
+++ b/solution.py
@@ -39,13 +39,13 @@
 
 
 def kernel(
-    tok_hbm, wl_hbm, wr_hbm, tgt_hbm,
+    tok_hbm, w_ref, tgt_hbm,
     tg_out, lg_out, rg_out,
-    tok_raw, tgt_raw, w_raw, tokT, tgtT, stage, stage2, stage3,
+    tok_raw, tgt_raw, tokT, tgtT, stage, stage2, stage3,
     gath, wfull, lw, lwT, rw, rwT,
     gp, fsend, frecv, bsend, brecv, lgrad, rgrad,
     rs0, rs_x, rs2, rs_z,
-    in_sem, w_sem, agz_s, agz_r, agx_s, agx_r, agc_s, agc_r,
+    in_sem, agz_s, agz_r, agx_s, agx_r, agc_s, agc_r,
     f_s, f_r, b_s, b_r, q_s, q_r, rx_s, rx_r, rz_s, rz_r, qx_s, qx_r, qz_s, qz_r,
 ):
     dp, mp = lax.axis_index("dp"), lax.axis_index("mp")
@@ -76,23 +76,17 @@
     for dev in peers:
         pl.semaphore_signal(barrier, inc=1, device_id=dev, device_id_type=MESH)
 
-    def w_in(f):
-        return pltpu.make_async_copy((wl_hbm, wr_hbm)[f], w_raw.at[f], w_sem.at[f])
-
     def tok_in(c):
         return pltpu.make_async_copy(tok_hbm.at[aligned(c, TC)], tok_raw.at[c], in_sem.at[0, c])
 
     def tgt_in(c):
         return pltpu.make_async_copy(tgt_hbm.at[aligned(c, TC)], tgt_raw.at[c], in_sem.at[1, c])
 
-    for f in (0, 1):
-        w_in(f).start()
     loop(0, CH, lambda c: tok_in(c).start())
     loop(0, CH, lambda c: tgt_in(c).start())
     for f in (0, 1):
-        w_in(f).wait()
         for h in (0, 1):
-            gath[f, h, core, x, z] = w_raw[f, 32 * h : 32 * h + 32].astype(BF)
+            gath[f, h, core, x, z] = w_ref[f, h]
     pl.semaphore_wait(barrier, len(peers))
 
     def ag_z(f, h, o):
@@ -274,28 +268,34 @@
     def send_back(c):
         loop(0, 7, lambda i: bwd_copy(c, first(i)).start())
 
+    def sent(copy, u):
+        loop(1, 8, lambda k: copy(u, k).wait_send())
+
     def turn(c):
         targets_ready(c)
-        loop(1, 8, lambda k: fwd_copy(c, k).wait_recv())
 
         @pl.when(c < 2)
         def _():
             tokens_ready(c + 2)
+            sent(fwd_copy, 2 * c)
             forward(c + 2)
+
+        loop(1, 8, lambda k: fwd_copy(c, k).wait_recv())
+        right(c)
+
+        @pl.when(c == 0)
+        def _():
+            sent(fwd_copy, 1)
+            send_back(0)
+
+        @pl.when(c == 1)
+        def _():
+            sent(bwd_copy, 0)
+            send_back(1)
 
         @pl.when(c == 2)
         def _():
-            send_back(1)
-
-        right(c)
-
-        @pl.when(c == 0)
-        def _():
-            send_back(0)
-
-        @pl.when(c == 2)
-        def _():
-            loop(1, 8, lambda k: bwd_copy(0, k).wait_recv())
+            sent(fwd_copy, 3)
             send_back(2)
 
     loop(0, CH, turn)
@@ -372,18 +372,21 @@
     for q in range(4):
         pieces(1, q, rgrad)
     loop(1, 8, lambda k: rx_copy(k).start())
+    loop(1, 8, lambda k: bwd_copy(0, k).wait_recv())
     left(0)
-    loop(1, 8, lambda k: bwd_copy(1, k).wait_recv())
+    sent(bwd_copy, 1)
     send_quarter(0)
     send_quarter(1)
+    send_quarter(2)
+    loop(1, 8, lambda k: bwd_copy(1, k).wait_recv())
     loop(1, 8, lambda k: rx_copy(k).wait_recv())
     for q in range(4):
         add_first(1, q)
     for o in (1, 2, 3):
         rz_copy(o).start()
     left(1)
+    sent(bwd_copy, 2)
     loop(1, 8, lambda k: bwd_copy(2, k).wait_recv())
-    send_quarter(2)
     left(2)
     for o in (1, 2, 3):
         rz_copy(o).wait_recv()
@@ -391,9 +394,10 @@
         add_last(1, q, rg_out)
 
     def quarter(q):
+        if q == 0:
+            sent(quarter_copy, 0)
+            send_quarter(3)
         loop(1, 8, lambda k: quarter_copy(q, k).wait_recv())
-        if q == 0:
-            send_quarter(3)
         left_part(LAST, 4 * q, 4 * q + 4)
         pieces(0, q, lgrad)
         loop(1, 8, lambda k: qx_copy(q, k).start())
@@ -404,12 +408,10 @@
         for o in (1, 2, 3):
             qz_copy(q, o).start()
 
-    quarter(0)
-    quarter(1)
+    for q in range(4):
+        quarter(q)
     second(0)
-    quarter(2)
     second(1)
-    quarter(3)
     second(2)
     left_out(LAST)
     second(3)
@@ -429,23 +431,13 @@
     for o in (1, 2, 3):
         rz_copy(o).wait_send()
 
-    def drain(c):
-        loop(1, 8, lambda k: fwd_copy(c, k).wait_send())
-
-    loop(0, CH, drain)
-
-    def drain_back(c):
-        loop(1, 8, lambda k: bwd_copy(c, k).wait_send())
-
-    loop(0, LAST, drain_back)
-
     def drain_quarter(q):
-        loop(1, 8, lambda k: quarter_copy(q, k).wait_send())
         loop(1, 8, lambda k: qx_copy(q, k).wait_send())
         for o in (1, 2, 3):
             qz_copy(q, o).wait_send()
 
     loop(0, 4, drain_quarter)
+    loop(1, 4, lambda q: sent(quarter_copy, q))
 
 
 def step(tokens, left_factor, right_factor, target):
@@ -455,7 +447,7 @@
     vmem = pl.BlockSpec(memory_space=pltpu.VMEM)
     sq = (128, 128)
     scratch = [
-        V((CH, TC, 16, 128), BF), V((CH, TC, 16, 128), BF), V((2, 64, 128), F32),
+        V((CH, TC, 16, 128), BF), V((CH, TC, 16, 128), BF),
         V((CH, 16, 128, TC), BF), V((CH, 16, 128, TC), BF),
         V((TC * 16, 128), F32), V((16 * 128, TC), F32), V((TC * 16, 128), F32),
         V((2, 2, 2, 4, 4, 32, 128), BF), V((8, 2) + sq, F32),
@@ -466,11 +458,14 @@
         V((8, 2) + sq, F32), V((8, 2) + sq, F32),
         V((2, 2, 4, 4, 4, 16, 128), BF), V((2, 7, 4, 4, 16, 128), BF),
         V((2, 4, 4, 16, 128), BF), V((2, 3, 4, 16, 128), BF),
-        D((2, CH)), D((2,)),
+        D((2, CH)),
         D((2, 2, 3)), D((2, 2, 3)), D((2, 2, 3)), D((2, 2, 3)), D((2, 2, 4)), D((2, 2, 4)),
         D((CH, 7)), D((CH, 7)), D((CH, 7)), D((CH, 7)), D((4, 7)), D((4, 7)),
         D((7,)), D((7,)), D((3,)), D((3,)), D((4, 7)), D((4, 7)), D((4, 3)), D((4, 3)),
     ]
+    which = lax.broadcasted_iota(jnp.int32, (2, 16, 4, 128), 0)
+    factors = jnp.where(which == 0, left_factor[None], right_factor[None])
+    factors = factors.astype(BF).reshape(2, 2, 32, 128)
     tg, lg, rg = pl.pallas_call(
         kernel,
         name="monarch",
@@ -479,13 +474,13 @@
             jax.ShapeDtypeStruct((64, 128), F32),
             jax.ShapeDtypeStruct((64, 128), F32),
         ),
-        in_specs=[hbm, hbm, hbm, hbm],
+        in_specs=[hbm, vmem, hbm],
         out_specs=(vmem, vmem, vmem),
         scratch_shapes=scratch,
         compiler_params=pltpu.CompilerParams(
             collective_id=0, has_side_effects=True, vmem_limit_bytes=51 << 20
         ),
-    )(tokens, left_factor.reshape(64, 128), right_factor.reshape(64, 128), target)
+    )(tokens, factors, target)
     return tg, lg.reshape(16, 4, 128), rg.reshape(16, 4, 128)
 
 

time: 138 us -> 135 us (0.978)
  Pallas kernels: 133 us -> 131 us
  local copies, waits for them, and re-layouts: 4.06 us -> 2.55 us
    pallas_call x1, Pallas kernels: 133 us -> 131 us  [step(): pl.pallas_call(kernel, name='monarch', out_shape=(jax.ShapeDtypeStruct((C...]
    unnamed x7 -> x3, local copies, waits for them, and re-layouts: 4.06 us -> 2.55 us
where the time goes in v3:
time: 135 us
  Pallas kernels  131 us (97%)
  local copies, waits for them, and re-layouts  2.55 us (2%)
    pallas_call x1, Pallas kernels, step(): pl.pallas_call(kernel, name='monarch', out_shape=(jax.ShapeDtypeStruct((C...  131 us

profile of v3, /device:TPU:1, one launch (start us, length us, event | category | flops | bytes accessed | tf_op | source)
XLA Modules:
  0.0 134.9 jit_solution(11164960624519406462)
XLA Ops:
  0.6 0.9 select_convert_fusion.w_ref
  1.5 130.9 %monarch.1 = (bf16[512,16,128]{2,1,0:T(8,128)(2,1)S(1)}, f32[64,128]{1,0:T(8,128)S(1)}, f32[64,128]{1,0:T(8,128)S(1)}) custom-call(bf16[512,16,128]{2,1,0:T(8,128)(2,1)} %tok_hbm.1, bf16[2,2,32,128]{3,2,1,0:T(8,128)(2,1)S(1)} %select_convert_fusion.w_ref, bf16[512,16,128]{2,1,0:T(8,128)(2,1)} %tgt_hbm.1), custom_call_target="tpu_custom_call" | custom-call | tf_op jit(solution)/shard_map/monarch/pallas_call | solution.py:469
  132.4 1.3 copy.10
  133.7 0.6 copy.11
  134.3 0.6 copy.12
  (1 shorter events, 0.0 us)

commit v4 on v3

--- a/solution.py
+++ b/solution.py
@@ -40,7 +40,7 @@
 
 def kernel(
     tok_hbm, w_ref, tgt_hbm,
-    tg_out, lg_out, rg_out,
+    tg_out, grads_out,
     tok_raw, tgt_raw, tokT, tgtT, stage, stage2, stage3,
     gath, wfull, lw, lwT, rw, rwT,
     gp, fsend, frecv, bsend, brecv, lgrad, rgrad,
@@ -385,13 +385,21 @@
     for o in (1, 2, 3):
         rz_copy(o).start()
     left(1)
+    for f in (0, 1):
+        for h in (0, 1):
+            for o in (1, 2, 3):
+                ag_z(f, h, o).wait_send()
+                ag_x(f, h, o).wait_send()
+            for o in (0, 1, 2, 3):
+                ag_c(f, h, o).wait_send()
+    loop(1, 8, lambda k: rx_copy(k).wait_send())
     sent(bwd_copy, 2)
     loop(1, 8, lambda k: bwd_copy(2, k).wait_recv())
     left(2)
     for o in (1, 2, 3):
-        rz_copy(o).wait_recv()
-    for q in range(4):
-        add_last(1, q, rg_out)
+        rz_copy(o).wait()
+    for q in range(4):
+        add_last(1, q, grads_out.at[1])
 
     def quarter(q):
         if q == 0:
@@ -414,30 +422,18 @@
     second(1)
     second(2)
     left_out(LAST)
+    loop(1, 4, lambda q: sent(quarter_copy, q))
+    loop(0, 3, lambda q: sent(qx_copy, q))
     second(3)
     for q in range(4):
         for o in (1, 2, 3):
             qz_copy(q, o).wait_recv()
-        add_last(0, q, lg_out)
-
-    for f in (0, 1):
-        for h in (0, 1):
-            for o in (1, 2, 3):
-                ag_z(f, h, o).wait_send()
-                ag_x(f, h, o).wait_send()
-            for o in (0, 1, 2, 3):
-                ag_c(f, h, o).wait_send()
-    loop(1, 8, lambda k: rx_copy(k).wait_send())
-    for o in (1, 2, 3):
-        rz_copy(o).wait_send()
-
-    def drain_quarter(q):
-        loop(1, 8, lambda k: qx_copy(q, k).wait_send())
+        add_last(0, q, grads_out.at[0])
+
+    sent(qx_copy, 3)
+    for q in range(4):
         for o in (1, 2, 3):
             qz_copy(q, o).wait_send()
-
-    loop(0, 4, drain_quarter)
-    loop(1, 4, lambda q: sent(quarter_copy, q))
 
 
 def step(tokens, left_factor, right_factor, target):
@@ -466,22 +462,22 @@
     which = lax.broadcasted_iota(jnp.int32, (2, 16, 4, 128), 0)
     factors = jnp.where(which == 0, left_factor[None], right_factor[None])
     factors = factors.astype(BF).reshape(2, 2, 32, 128)
-    tg, lg, rg = pl.pallas_call(
+    tg, grads = pl.pallas_call(
         kernel,
         name="monarch",
         out_shape=(
             jax.ShapeDtypeStruct((CH * TC, 16, 128), BF),
-            jax.ShapeDtypeStruct((64, 128), F32),
-            jax.ShapeDtypeStruct((64, 128), F32),
+            jax.ShapeDtypeStruct((2, 64, 128), F32),
         ),
         in_specs=[hbm, vmem, hbm],
-        out_specs=(vmem, vmem, vmem),
+        out_specs=(vmem, vmem),
         scratch_shapes=scratch,
         compiler_params=pltpu.CompilerParams(
             collective_id=0, has_side_effects=True, vmem_limit_bytes=51 << 20
         ),
     )(tokens, factors, target)
-    return tg, lg.reshape(16, 4, 128), rg.reshape(16, 4, 128)
+    lg, rg = grads.reshape(2, 16, 4, 128)
+    return tg, lg, rg
 
 
 def solution(mesh):

time: 135 us -> 134 us (level)
  no operation moved by 1% of the time
where the time goes in v4:
time: 134 us
  Pallas kernels  130 us (97%)
  local copies, waits for them, and re-layouts  1.95 us (1%)
    pallas_call x1, Pallas kernels, step(): pl.pallas_call(kernel, name='monarch', out_shape=(jax.ShapeDtypeStruct((C...  130 us

profile of v4, /device:TPU:1, one launch (start us, length us, event | category | flops | bytes accessed | tf_op | source)
XLA Modules:
  0.0 134.0 jit_solution(6989583793347383925)
XLA Ops:
  0.6 0.9 select_convert_fusion.w_ref
  1.5 130.5 %monarch.1 = (bf16[512,16,128]{2,1,0:T(8,128)(2,1)S(1)}, f32[2,64,128]{2,1,0:T(8,128)S(1)}) custom-call(bf16[512,16,128]{2,1,0:T(8,128)(2,1)} %tok_hbm.1, bf16[2,2,32,128]{3,2,1,0:T(8,128)(2,1)S(1)} %select_convert_fusion.w_ref, bf16[512,16,128]{2,1,0:T(8,128)(2,1)} %tgt_hbm.1), custom_call_target="tpu_custom_call" | custom-call | tf_op jit(solution)/shard_map/monarch/pallas_call | solution.py:465
  132.0 0.6 fusion
  132.6 1.3 copy.8
  (1 shorter events, 0.0 us)

commit v5 on v4

--- a/solution.py
+++ b/solution.py
@@ -122,7 +122,7 @@
             ag_c(f, h, o).wait_recv()
 
     def spread(raw, outT, c):
-        stage[...] = raw[c].astype(F32).reshape(TC * 16, 128)
+        stage[: TC * 16, :] = raw[c].astype(F32).reshape(TC * 16, 128)
 
         def one(n):
             rows = stage[pl.ds(n, TC, stride=16), :]
@@ -408,7 +408,7 @@
         loop(1, 8, lambda k: quarter_copy(q, k).wait_recv())
         left_part(LAST, 4 * q, 4 * q + 4)
         pieces(0, q, lgrad)
-        loop(1, 8, lambda k: qx_copy(q, k).start())
+        loop(0, 7, lambda i: qx_copy(q, lax.rem(i + 1, 7) + 1).start())
 
     def second(q):
         loop(1, 8, lambda k: qx_copy(q, k).wait_recv())
@@ -445,7 +445,7 @@
     scratch = [
         V((CH, TC, 16, 128), BF), V((CH, TC, 16, 128), BF),
         V((CH, 16, 128, TC), BF), V((CH, 16, 128, TC), BF),
-        V((TC * 16, 128), F32), V((16 * 128, TC), F32), V((TC * 16, 128), F32),
+        V((TC * 16 + 16, 128), F32), V((17 * 128, TC), F32), V((TC * 16 + 16, 128), F32),
         V((2, 2, 2, 4, 4, 32, 128), BF), V((8, 2) + sq, F32),
         V((16,) + sq, BF), V((16,) + sq, BF), V((16,) + sq, BF), V((16,) + sq, BF),
         V((CH, 16, 128, TC), F32),

time: 134 us -> 134 us (level)
  no operation moved by 1% of the time
where the time goes in v5:
time: 134 us
  Pallas kernels  130 us (97%)
  local copies, waits for them, and re-layouts  1.95 us (1%)
    pallas_call x1, Pallas kernels, step(): pl.pallas_call(kernel, name='monarch', out_shape=(jax.ShapeDtypeStruct((C...  130 us

profile of v5, /device:TPU:1, one launch (start us, length us, event | category | flops | bytes accessed | tf_op | source)
XLA Modules:
  0.0 133.8 jit_solution(11800230737207884648)
XLA Ops:
  0.6 0.9 select_convert_fusion.w_ref
  1.5 130.3 %monarch.1 = (bf16[512,16,128]{2,1,0:T(8,128)(2,1)S(1)}, f32[2,64,128]{2,1,0:T(8,128)S(1)}) custom-call(bf16[512,16,128]{2,1,0:T(8,128)(2,1)} %tok_hbm.1, bf16[2,2,32,128]{3,2,1,0:T(8,128)(2,1)S(1)} %select_convert_fusion.w_ref, bf16[512,16,128]{2,1,0:T(8,128)(2,1)} %tgt_hbm.1), custom_call_target="tpu_custom_call" | custom-call | tf_op jit(solution)/shard_map/monarch/pallas_call | solution.py:465
  131.8 0.6 fusion
  132.5 1.3 copy.8
  (1 shorter events, 0.0 us)
